TPU v7x, 128 devices: a whole 4x4x4 slice. The times are simulated.
128 devices in a mesh: tm: 8 (over x_hi, y), chan: 16 (over z, x_lo, core).
Axes of the slice: x: 4 (x_hi: 2, x_lo: 2; x = x_hi * 2 + x_lo), y: 4, z: 4, core: 2. Of those that a mesh axis runs over, the one named last changes fastest.
Arguments:
- voltages: bfloat16 [2048, 131072], P('chan', 'tm'), may hold values from -6 to 6
- filter_taps: float32 [4, 16384], replicated, may hold values from -2 to 2
- delays: int32 [2048], P('chan'), may hold values from 0 to 4095
- dead_inputs: int32 [2048], P('chan'), may hold values 0 or 1
Outputs:
- visibilities: bfloat16 [128, 2048, 2048], P(('tm', 'chan'))
All inputs are finite; a program needn't handle non-finite values. No bound on the sum of `dead_inputs` on one device may be relied on, other than what follows from the above.
Results may differ from a plain program's by a relative error of at most 0.0056.
Values may be sent and summed in bfloat16 or wider, within the bound.
A program may use at most 128 MiB of HBM per device.

v0:
```python
import jax
import jax.numpy as jnp
from jax import lax
from jax.sharding import PartitionSpec as P

R = 128


two_pi = 6.283185307179586


def shifted(value, axis, steps):
    count = lax.axis_size(axis)
    initial, last = (max(0, -steps), min(count, count - steps))
    return lax.ppermute(value, axis, [(source, source + steps) for source in range(initial, last)])


def dft_tables(radix):
    length = radix * radix
    indices = jnp.arange(radix, dtype=jnp.int32)
    outer = indices[:, None] * indices[None, :]
    angles = two_pi / radix * (outer % radix).astype(jnp.float32)
    first_section = jnp.stack([jnp.cos(angles), -jnp.sin(angles)], axis=2).astype(jnp.bfloat16)
    twist = two_pi / length * outer.astype(jnp.float32)
    half_cos = jnp.cos(angles[:, : radix // 2])
    half_sin = jnp.sin(angles[:, : radix // 2])
    second_section = jnp.stack(
        [jnp.stack([half_cos, -half_sin], axis=1), jnp.stack([half_sin, half_cos], axis=1)], axis=0
    ).astype(jnp.bfloat16)
    return (first_section, jnp.cos(twist), jnp.sin(twist), second_section)


def channelise(filtered, delays, dead_inputs, radix):
    signals_here, spectra_here, length = filtered.shape
    first_section, twist_cos, twist_sin, second_section = dft_tables(radix)
    blocks = filtered.reshape(signals_here, spectra_here, radix, radix)
    partial_sums = jnp.einsum(
        "gtab,akp->gtkpb", blocks, first_section, preferred_element_type=jnp.float32
    )
    real_part = partial_sums[:, :, :, 0, :]
    imag_part = partial_sums[:, :, :, 1, :]
    turned = jnp.stack(
        [
            real_part * twist_cos + imag_part * twist_sin,
            imag_part * twist_cos - real_part * twist_sin,
        ],
        axis=3,
    ).astype(jnp.bfloat16)
    spectra = jnp.einsum(
        "gtkpb,pbsm->stmkg", turned, second_section, preferred_element_type=jnp.float32
    )
    spectra = spectra.reshape(2, spectra_here, length // 2, signals_here)
    channels = jnp.arange(length // 2, dtype=jnp.int32)
    phases = two_pi / length * (channels[:, None] * delays[None, :] % length).astype(jnp.float32)
    weight = (1 - dead_inputs).astype(jnp.float32) / radix
    rot_cos = jnp.cos(phases) * weight
    rot_sin = jnp.sin(phases) * weight
    return jnp.stack(
        [spectra[0] * rot_cos - spectra[1] * rot_sin, spectra[0] * rot_sin + spectra[1] * rot_cos],
        axis=0,
    ).astype(jnp.bfloat16)


def filter_blocks(extended, filter_taps, count, reach_back):
    filtered = filter_taps[0][None, None, :] * extended[:, reach_back : reach_back + count].astype(
        jnp.float32
    )
    for tap_index in range(1, filter_taps.shape[0]):
        filtered = filtered + filter_taps[tap_index][None, None, :] * extended[
            :, reach_back - tap_index : reach_back - tap_index + count
        ].astype(jnp.float32)
    return filtered.astype(jnp.bfloat16)


def pair_products(row_data, col_data):
    power = jnp.einsum(
        "ijptcs,ikptcu->jsku", row_data, col_data, preferred_element_type=jnp.float32
    )
    phase_part = jnp.einsum(
        "ijtcs,iktcu->jsku",
        row_data[:, :, 1],
        col_data[:, :, 0],
        preferred_element_type=jnp.float32,
    )
    phase_part = phase_part - jnp.einsum(
        "ijtcs,iktcu->jsku",
        row_data[:, :, 0],
        col_data[:, :, 1],
        preferred_element_type=jnp.float32,
    )
    return (power, phase_part)


def shards(voltages, filter_taps, delays, dead_inputs):
    signals_here, samples_here = voltages.shape
    length = filter_taps.shape[1]
    spectra_here = samples_here // length
    own_blocks = voltages.reshape(signals_here, spectra_here, length)
    reach_back = filter_taps.shape[0] - 1
    n_time = lax.axis_size("tm")
    n_chan = lax.axis_size("chan")
    sources = (spectra_here + reach_back - 1) // spectra_here
    history = []
    for offset in range(sources, 0, -1):
        needed = min(spectra_here, reach_back - (offset - 1) * spectra_here)
        history.append(shifted(own_blocks, "tm", offset))
    extended = jnp.concatenate(history + [own_blocks], axis=1)
    filtered = filter_blocks(extended, filter_taps, spectra_here, reach_back)
    spectra = channelise(filtered, delays, dead_inputs, R)
    count = spectra.shape[1]
    narrow = spectra.shape[3]
    received = lax.all_to_all(
        spectra[None], ("tm", "chan"), split_axis=3, concat_axis=0, tiled=True
    )
    received = received.reshape(n_time, n_chan, 2, count, -1, narrow)
    fine_count = received.shape[4]
    scale = 1.0 / (fine_count * received.shape[0] * received.shape[3])
    width_here = received.shape[5]
    quarter = n_chan // 4
    width = quarter * width_here
    grid = [[None] * 4 for row_index in range(4)]
    for row_index in range(4):
        row_data = received[:, row_index * quarter : (row_index + 1) * quarter]
        for col_index in range(row_index + 1):
            col_data = received[:, col_index * quarter : (col_index + 1) * quarter]
            power, phase_part = pair_products(row_data, col_data)
            power = power.reshape(width, width)
            phase_part = phase_part.reshape(width, width)
            if row_index == col_index:
                grid[row_index][col_index] = jnp.tril(power) + jnp.triu(phase_part, 1)
            else:
                grid[row_index][col_index] = power
                grid[col_index][row_index] = -phase_part.T
    packed = jnp.block(grid)
    return (packed * scale).astype(jnp.bfloat16)[None]


def solution(mesh):
    in_specs = (P("chan", "tm"), P(), P("chan"), P("chan"))
    out_specs = P(("tm", "chan"), None, None)
    return jax.shard_map(shards, mesh=mesh, in_specs=in_specs, out_specs=out_specs, check_vma=False)
```

profile of v0, /device:TPU:1, one launch (start us, length us, event | category | flops | bytes accessed | tf_op | source)
XLA Modules:
  0.0 709.9 jit_solution(14072150032741308023)
XLA Ops:
  0.0 6.1 collective-permute-start
  6.1 4.5 collective-permute-start.1
  10.6 5.4 collective-permute-start.2
  19.5 74.1 %collective-permute-done = bf16[128,1,16384]{2,0,1:T(8,128)(2,1)} collective-permute-done((bf16[128,1,16384]{2,0,1:T(8,128)(2,1)}, bf16[128,1,16384]{2,0,1:T(8,128)(2,1)}, u32[]{:S(2)}, u32[]{:S(2)}) %collective-permute-start) | collective-permute-done | bytes 4194336 | tf_op jit(solution)/shard_map/ppermute | solution.py:15
  93.6 89.9 %collective-permute-done.1 = bf16[128,1,16384]{2,0,1:T(8,128)(2,1)} collective-permute-done((bf16[128,1,16384]{2,0,1:T(8,128)(2,1)}, bf16[128,1,16384]{2,0,1:T(8,128)(2,1)}, u32[]{:S(2)}, u32[]{:S(2)}) %collective-permute-start.1) | collective-permute-done | bytes 4194336 | tf_op jit(solution)/shard_map/ppermute | solution.py:15
  183.5 7.1 collective-permute-done.2
  190.6 7.5 %fusion.12 = bf16[16,8,128,128]{3,1,2,0:T(8,128)(2,1)S(1)} fusion(bf16[128,1,16384]{2,0,1:T(8,128)(2,1)} %collective-permute-done.2, bf16[128,1,16384]{2,0,1:T(8,128)(2,1)} %collective-permute-done.1, bf16[128,1,16384]{2,0,1:T(8,128)(2,1)} %collective-permute-done, bf16[128,16384]{1,0:T(8,128)(2,1)} %param.4, f32[16384]{0:T(1024)S(1)} %bitcast.516, ...), kind=kLoop, calls=%fused_computation.21 | loop fusion | flops 25165824 | bytes 21233664
  199.3 2.3 convolution_bitcast_fusion
  201.7 2.5 fusion.10
  204.2 2.8 fusion.20
  207.0 4.2 fusion.152
  211.2 5.5 copy.184
  216.6 5.4 copy.185
  222.1 19.4 %fusion.14 = (bf16[1,8192,128]{2,1,0:T(8,128)(2,1)S(1)}, bf16[1,8192,128]{2,1,0:T(8,128)(2,1)S(1)}) fusion(f32[1,1,64,128,128]{4,3,2,1,0:T(8,128)} %copy.185, f32[1,1,64,128,128]{4,3,2,1,0:T(8,128)} %copy.184, f32[128]{0:T(128)S(1)} %convert_multiply_fusion.1, s32[128]{0:T(128)S(1)} %copy-done.33), kind=kLoop, calls=%fused_computation.30 | loop fusion | flops 25165824 | bytes 12583936 | tf_op jit(solution)/shard_map/convert.3
  241.9 35.5 %copy.114 = bf16[1,2,1,8192,128]{4,1,2,0,3:T(2,128)(2,1)S(1)} copy(bf16[1,2,1,8192,128]{4,3,2,1,0:T(8,128)(2,1)S(1)} %pad_maximum_fusion.1) | data formatting | bytes 8388608 | tf_op jit(solution)/shard_map/stack | solution.py:58
  277.4 314.7 %all_to_all.15 = bf16[1,2,1,8192,128]{4,1,2,0,3:T(2,128)(2,1)S(1)} all-to-all(bf16[1,2,1,8192,128]{4,1,2,0,3:T(2,128)(2,1)S(1)} %copy.114), channel_id=1, replica_groups=mesh['tm'=8,'chan'=16] {'tm','chan'}, dimensions={3} | all-to-all | bytes 8388608 | tf_op jit(solution)/shard_map/all_to_all | solution.py:112
  610.7 2.4 copy.396
  613.1 3.0 copy.135
  618.4 3.6 convolution_bitcast_fusion.21
  622.0 3.5 convolution_bitcast_fusion.13
  631.9 2.4 dot_general.151
  634.3 3.6 convolution_bitcast_fusion.6
  638.0 3.4 convolution_bitcast_fusion.5
  645.0 2.5 copy.120
  647.5 3.7 fusion.24
  660.8 2.5 copy.132
  663.3 3.7 fusion.26
  673.0 2.6 copy.137
  675.5 3.9 fusion.28
  683.5 2.8 fusion.30
  692.9 4.4 fusion
  697.3 12.2 %copy.142 = bf16[1,2048,2048]{2,1,0:T(8,128)(2,1)} copy(bf16[1,2048,2048]{1,2,0:T(8,128)(2,1)} %fusion) | data formatting | bytes 16777216 | tf_op jit(solution)/shard_map/convert_element_type | solution.py:135
  (128 shorter events, 62.1 us)
Async XLA Ops:
  0.0 93.6 %collective-permute-start = (bf16[128,1,16384]{2,0,1:T(8,128)(2,1)}, bf16[128,1,16384]{2,0,1:T(8,128)(2,1)}, u32[]{:S(2)}, u32[]{:S(2)}) collective-permute-start(bf16[128,1,16384]{2,0,1:T(8,128)(2,1)} %bitcast.498), channel_id=1, source_target_pairs={{0,16},{16,32},{32,48},{48,64},{64,80},{80,96},{96,112},{1,17},{17... | collective-permute-start | bytes 12582920 | tf_op jit(solution)/shard_map/ppermute | solution.py:15
  6.1 177.4 %collective-permute-start.1 = (bf16[128,1,16384]{2,0,1:T(8,128)(2,1)}, bf16[128,1,16384]{2,0,1:T(8,128)(2,1)}, u32[]{:S(2)}, u32[]{:S(2)}) collective-permute-start(bf16[128,1,16384]{2,0,1:T(8,128)(2,1)} %bitcast.499), channel_id=1, source_target_pairs={{0,32},{16,48},{32,64},{48,80},{64,96},{80,112},{1,33},{17,49},{33... | collective-permute-start | bytes 12582920 | tf_op jit(solution)/shard_map/ppermute | solution.py:15
  10.6 180.0 %collective-permute-start.2 = (bf16[128,1,16384]{2,0,1:T(8,128)(2,1)}, bf16[128,1,16384]{2,0,1:T(8,128)(2,1)}, u32[]{:S(2)}, u32[]{:S(2)}) collective-permute-start(bf16[128,1,16384]{2,0,1:T(8,128)(2,1)} %bitcast.500), channel_id=1, source_target_pairs={{0,48},{16,64},{32,80},{48,96},{64,112},{1,49},{17,65},{33,81},{49... | collective-permute-start | bytes 12582920 | tf_op jit(solution)/shard_map/ppermute | solution.py:15
  216.6 5.4 copy-start.33
  595.7 7.9 %copy-start.2 = (bf16[8,4,1,1,64,128]{5,4,2,1,0,3:T(8,128)(2,1)}, bf16[8,4,1,1,64,128]{5,4,2,1,0,3:T(8,128)(2,1)S(1)}, u32[]{:S(2)}) copy-start(bf16[8,4,1,1,64,128]{5,4,2,1,0,3:T(8,128)(2,1)S(1)} %get-tuple-element.17) | copy-start | bytes 1572868
  618.4 7.0 copy-start.21
  618.4 7.0 copy-start.23
  625.4 4.7 copy-start.18
  634.3 7.0 copy-start.20
  634.3 7.0 copy-start.22
  637.9 5.2 copy-start
  637.9 5.2 copy-start.3
  647.5 3.7 copy-start.1
  647.5 3.7 copy-start.12
  651.3 2.3 copy-start.11
  653.5 3.6 copy-start.9
  657.1 2.2 copy-start.8
  663.3 3.7 copy-start.6
  667.0 2.2 copy-start.5
  669.2 2.3 copy-start.7
  671.5 8.0 %copy-start.4 = (f32[4,128,4,128]{3,1,2,0:T(8,128)S(1)}, f32[4,128,4,128]{3,1,2,0:T(8,128)}, u32[]{:S(2)}) copy-start(f32[4,128,4,128]{3,1,2,0:T(8,128)} %convolution_bitcast_fusion.7) | copy-start | bytes 3145732
  679.5 2.2 copy-start.10
  681.7 4.6 copy-start.13
  682.1 4.1 copy-start.14
  683.5 2.8 copy-start.15
  683.5 2.8 copy-start.30
  686.3 1.8 copy-start.26
  686.3 2.1 copy-start.31
  688.4 1.5 copy-start.24
  688.4 1.9 copy-start.25
  688.4 2.2 copy-start.32
  690.6 1.9 copy-start.29
  (5 other events, 6.7 us)
where the time goes:
time: 720 us; the launch traced here: 710 us
  blocking collectives  315 us (44%)
  waiting for transfers between devices  171 us (24%)
  local copies, waits for them, and re-layouts  112 us (16%)
  matrix products  57.9 us (8%)
  other arithmetic  37.5 us (5%)
  starting transfers between devices  16 us (2%)
    all_to_all x1, blocking collectives, shards(): lax.all_to_all(spectra[None], ('tm', 'chan'), split_axis=3, concat_axis=0...  315 us
    ppermute x3, waiting for transfers between devices, shifted(): lax.ppermute(value, axis, [(source, source + steps) for source in range(i...  171 us
    another operation x1, local copies, waits for them, and re-layouts, channelise(): jnp.stack([spectra[0] * rot_cos - spectra[1] * rot_sin, spectra[0] * rot_...  35.5 us
    dot_general x10, matrix products, pair_products(): jnp.einsum('ijptcs,ikptcu->jsku', row_data, col_data, preferred_element_t...  31.6 us
    another operation x2, other arithmetic  19.7 us
    dot_general x7, local copies, waits for them, and re-layouts, pair_products(): jnp.einsum('ijptcs,ikptcu->jsku', row_data, col_data, preferred_element_t...  16 us
    ppermute x3, starting transfers between devices, shifted(): lax.ppermute(value, axis, [(source, source + steps) for source in range(i...  16 us
    unnamed x76, local copies, waits for them, and re-layouts  14.6 us
  transfers between devices with their start and end apart: 3, of which 3 were waited for; matrix products, arithmetic and copies ran while one was open for 0% of the time, Pallas kernels for 0%

commit v1 on v0

v1 whole, which is shorter than its diff:
```python
import functools

import jax
import jax.numpy as jnp
import numpy as np
from jax import lax
from jax.experimental import pallas as pl
from jax.experimental.pallas import tpu as pltpu
from jax.sharding import PartitionSpec as P

R = 128
HALF = R // 2
N_TIME = 8
N_CHAN = 16
MESH = pl.DeviceIdType.MESH
two_pi = 2.0 * np.pi


def dft_tables():
    indices = np.arange(R)
    outer = indices[:, None] * indices[None, :]
    angles = two_pi / R * (outer % R)
    cos, sin = np.cos(angles), np.sin(angles)
    first = np.concatenate([cos, -sin], axis=0)
    twist = two_pi / (R * R) * outer
    cos_m, sin_m = cos[:HALF], sin[:HALF]
    second = np.concatenate(
        [np.concatenate([cos_m, sin_m], axis=1), np.concatenate([-sin_m, cos_m], axis=1)], axis=0
    )
    return (
        jnp.asarray(first, jnp.bfloat16),
        jnp.asarray(np.cos(twist), jnp.float32),
        jnp.asarray(np.sin(twist), jnp.float32),
        jnp.asarray(second, jnp.bfloat16),
    )


def gather_times_kernel(volts, out, send_sem, recv_sem):
    share = out.shape[1]
    tm = lax.axis_index("tm")

    def source(owner):
        return volts.at[pl.ds(owner * share, share)]

    mine = pltpu.make_async_copy(source(tm), out.at[tm], recv_sem)
    mine.start()

    def send(step, carry):
        owner = lax.rem(tm + step, N_TIME)
        pltpu.make_async_remote_copy(
            src_ref=source(owner),
            dst_ref=out.at[tm],
            send_sem=send_sem,
            recv_sem=recv_sem,
            device_id={"tm": owner},
            device_id_type=MESH,
        ).start()
        return carry

    lax.fori_loop(1, N_TIME, send, 0)
    pltpu.make_async_copy(out, out, recv_sem).wait()
    most = out.at[pl.ds(0, N_TIME - 1)]
    pltpu.make_async_copy(most, most, send_sem).wait()


def channelise_kernel(volts, taps, first, twist_cos, twist_sin, second, rot, out, turned_rows):
    share = volts.shape[1]
    n_taps = taps.shape[0]
    low = lax.broadcasted_iota(jnp.int32, (HALF, R), 1) < HALF

    def one_signal(s, carry):
        spectra = []
        for t in range(N_TIME):
            filtered = taps[0] * volts[t, s].astype(jnp.float32)
            for j in range(1, min(n_taps, t + 1)):
                filtered = filtered + taps[j] * volts[t - j, s].astype(jnp.float32)
            sums = jnp.dot(
                first[...], filtered.astype(jnp.bfloat16), preferred_element_type=jnp.float32
            )
            real, imag = sums[:R], sums[R:]
            turned = jnp.concatenate(
                [
                    (real * twist_cos[...] + imag * twist_sin[...]).astype(jnp.bfloat16),
                    (imag * twist_cos[...] - real * twist_sin[...]).astype(jnp.bfloat16),
                ],
                axis=1,
            )
            raw = lax.dot_general(
                second[...],
                turned,
                (((1,), (1,)), ((), ())),
                preferred_element_type=jnp.float32,
            )
            rot_cos, rot_sin = rot[0, s], rot[1, s]
            spectra.append(
                (
                    raw[:HALF] * rot_cos - raw[HALF:] * rot_sin,
                    raw[:HALF] * rot_sin + raw[HALF:] * rot_cos,
                )
            )
            if t % 2 == 1:
                for part in range(2):
                    even, odd = spectra[t - 1][part], spectra[t][part]
                    lower = jnp.where(low, even, pltpu.roll(odd, HALF, 1))
                    upper = jnp.where(low, pltpu.roll(even, HALF, 1), odd)
                    tile = (t // 2) * 2 + part
                    for half, value in enumerate((lower, upper)):
                        row = ((tile * 2 + half) * share + s) * HALF
                        turned_rows[pl.ds(pl.multiple_of(row, HALF), HALF), :] = value
        return carry

    lax.fori_loop(0, share, one_signal, 0)

    def one_channel(m, carry):
        for half in range(2):
            for tile in range(N_TIME):
                base = (tile * 2 + half) * share * HALF
                rows = turned_rows[pl.ds(base + m, share, stride=HALF), :]
                out[2 * m + half, :, tile * R : (tile + 1) * R] = rows.astype(jnp.bfloat16)
        return carry

    lax.fori_loop(0, HALF, one_channel, 0)


def exchange_kernel(spectra, out, send_sem, recv_sem):
    groups, share, _ = spectra.shape
    tm, chan = lax.axis_index("tm"), lax.axis_index("chan")
    me = tm * N_CHAN + chan
    rows = pl.ds(pl.multiple_of((chan * N_TIME + tm) * share, share), share)
    pltpu.make_async_copy(spectra.at[me], out.at[rows], recv_sem).start()

    def send(step, carry):
        group = lax.rem(me + step, groups)
        pltpu.make_async_remote_copy(
            src_ref=spectra.at[group],
            dst_ref=out.at[rows],
            send_sem=send_sem,
            recv_sem=recv_sem,
            device_id={"tm": group // N_CHAN, "chan": lax.rem(group, N_CHAN)},
            device_id_type=MESH,
        ).start()
        return carry

    lax.fori_loop(1, groups, send, 0)
    pltpu.make_async_copy(out, out, recv_sem).wait()
    most = spectra.at[pl.ds(0, groups - 1)]
    pltpu.make_async_copy(most, most, send_sem).wait()


def correlate_kernel(scale, spectra, out, left):
    block = out.shape[0]
    depth = spectra.shape[1]
    i = pl.program_id(0)
    own = spectra[pl.ds(pl.multiple_of(i * block, block), block), :]
    left[0] = own
    for pair in range(depth // (2 * R)):
        real = slice(2 * pair * R, (2 * pair + 1) * R)
        imag = slice((2 * pair + 1) * R, (2 * pair + 2) * R)
        left[1, :, real] = own[:, imag]
        left[1, :, imag] = -own[:, real]

    def product(which, j):
        other = spectra[pl.ds(pl.multiple_of(j * block, block), block), :]
        return lax.dot_general(
            left[which], other, (((1,), (1,)), ((), ())), preferred_element_type=jnp.float32
        )

    def column(j, carry):
        which = (j > i).astype(jnp.int32)
        columns = pl.ds(pl.multiple_of(j * block, block), block)
        out[:, columns] = (product(which, j) * scale).astype(out.dtype)
        return carry

    lax.fori_loop(0, out.shape[1] // block, column, 0)
    shape = (block, block)
    lower = lax.broadcasted_iota(jnp.int32, shape, 0) >= lax.broadcasted_iota(jnp.int32, shape, 1)
    diagonal = pl.ds(pl.multiple_of(i * block, block), block)
    phase = (product(1, i) * scale).astype(out.dtype)
    out[:, diagonal] = jnp.where(lower, out[:, diagonal], phase)


def rotations(delays, dead_inputs):
    fine = two_pi / (R * R) * (delays[:, None] * jnp.arange(R, dtype=jnp.int32) % (R * R)).astype(jnp.float32)
    coarse = two_pi / R * (delays[:, None] * jnp.arange(HALF, dtype=jnp.int32) % R).astype(jnp.float32)
    weight = (1 - dead_inputs).astype(jnp.float32)[:, None] / R
    fine_cos, fine_sin = (jnp.cos(fine) * weight)[:, None, :], (jnp.sin(fine) * weight)[:, None, :]
    coarse_cos, coarse_sin = jnp.cos(coarse)[:, :, None], jnp.sin(coarse)[:, :, None]
    return jnp.stack(
        [coarse_cos * fine_cos - coarse_sin * fine_sin, coarse_sin * fine_cos + coarse_cos * fine_sin],
        axis=0,
    )


def shards(voltages, filter_taps, delays, dead_inputs):
    signals_here = voltages.shape[0]
    share = signals_here // N_TIME
    signals = signals_here * N_CHAN
    groups = N_TIME * N_CHAN
    depth = N_TIME * R
    anywhere = pl.BlockSpec(memory_space=pl.ANY)
    in_vmem = pl.BlockSpec(memory_space=pltpu.VMEM)
    sems = [pltpu.SemaphoreType.DMA, pltpu.SemaphoreType.DMA]

    gathered = pl.pallas_call(
        gather_times_kernel,
        out_shape=jax.ShapeDtypeStruct((N_TIME, share, R, R), jnp.bfloat16),
        in_specs=[anywhere],
        out_specs=anywhere,
        scratch_shapes=sems,
        compiler_params=pltpu.CompilerParams(has_side_effects=True),
        name="gather_times",
    )(voltages.reshape(signals_here, R, R))

    first = lax.axis_index("tm") * share
    rot = rotations(
        lax.dynamic_slice_in_dim(delays, first, share), lax.dynamic_slice_in_dim(dead_inputs, first, share)
    )
    spectra = pl.pallas_call(
        channelise_kernel,
        out_shape=jax.ShapeDtypeStruct((groups, share, depth), jnp.bfloat16),
        in_specs=[in_vmem] * 7,
        out_specs=in_vmem,
        scratch_shapes=[pltpu.VMEM((N_TIME * 2 * share * HALF, R), jnp.float32)],
        compiler_params=pltpu.CompilerParams(vmem_limit_bytes=40 * 2**20),
        name="channelise",
    )(gathered, filter_taps.reshape(-1, R, R), *dft_tables(), rot)

    everyone = pl.pallas_call(
        exchange_kernel,
        out_shape=jax.ShapeDtypeStruct((signals, depth), jnp.bfloat16),
        in_specs=[anywhere],
        out_specs=anywhere,
        scratch_shapes=sems,
        compiler_params=pltpu.CompilerParams(has_side_effects=True),
        name="exchange",
    )(spectra)

    block = 256
    scale = 1.0 / (HALF * N_TIME)
    return pl.pallas_call(
        functools.partial(correlate_kernel, scale),
        grid=(signals // block,),
        out_shape=jax.ShapeDtypeStruct((1, signals, signals), jnp.bfloat16),
        in_specs=[pl.BlockSpec((signals, depth), lambda i: (0, 0), pipeline_mode=pl.Buffered(1))],
        out_specs=pl.BlockSpec((None, block, signals), lambda i: (0, i, 0)),
        scratch_shapes=[pltpu.VMEM((2, block, depth), jnp.bfloat16)],
        compiler_params=pltpu.CompilerParams(vmem_limit_bytes=40 * 2**20),
        name="correlate",
    )(everyone)


def solution(mesh):
    in_specs = (P("chan", "tm"), P(), P("chan"), P("chan"))
    out_specs = P(("tm", "chan"), None, None)
    return jax.shard_map(shards, mesh=mesh, in_specs=in_specs, out_specs=out_specs, check_vma=False)
```

time: 720 us -> 229 us (0.32)
  the two profiles are of different devices: /device:TPU:1 before, /device:TPU:29 now
where the time goes in v1:
time: 229 us
  Pallas kernels  214 us (93%)
  local copies, waits for them, and re-layouts  13.5 us (6%)
    pallas_call x1, Pallas kernels, shards(): pl.pallas_call(exchange_kernel, out_shape=jax.ShapeDtypeStruct((signals,...  93.2 us
    pallas_call x1, Pallas kernels, shards(): pl.pallas_call(gather_times_kernel, out_shape=jax.ShapeDtypeStruct((N_TIM...  74.4 us
    pallas_call x1, Pallas kernels, shards(): pl.pallas_call(functools.partial(correlate_kernel, scale), grid=(signals...  26.4 us
    pallas_call x1, Pallas kernels, shards(): pl.pallas_call(channelise_kernel, out_shape=jax.ShapeDtypeStruct((groups,...  19.6 us
    unnamed x16, local copies, waits for them, and re-layouts  12.8 us

profile of v1, /device:TPU:29, one launch (start us, length us, event | category | flops | bytes accessed | tf_op | source)
XLA Modules:
  0.0 228.7 jit_solution(5657506811892036518)
XLA Ops:
  0.0 0.7 dynamic_slice.6
  0.7 0.7 convert_multiply_fusion
  1.5 0.1 cosine_multiply_fusion
  1.6 0.1 fusion.13
  1.7 1.0 copy.12
  2.7 0.3 multiply_subtract_fusion
  3.0 0.1 pad_maximum_fusion.rot
  3.1 5.4 %copy.9 = bf16[16,8,128,128]{3,2,1,0:T(8,128)(2,1)} copy(bf16[16,8,128,128]{3,1,2,0:T(8,128)(2,1)} %bitcast.8) | data formatting | bytes 8388608
  8.6 0.0 copy-start.3
  8.6 0.0 copy-start.4
  8.6 0.0 copy-start.5
  8.6 0.0 copy-start.6
  8.6 74.4 %gather_times.1.volts = bf16[8,16,128,128]{3,2,1,0:T(8,128)(2,1)} custom-call(bf16[128,128,128]{2,1,0:T(8,128)(2,1)} %bitcast.7), custom_call_target="tpu_custom_call" | custom-call | tf_op jit(solution)/shard_map/gather_times/pallas_call | solution.py:204
  83.0 0.0 copy-done.3
  83.0 0.0 copy-done.4
  83.0 0.0 copy-done.5
  83.0 0.0 copy-done.6
  83.0 0.0 copy-start.1
  83.0 2.2 copy-done.1
  85.2 19.6 %channelise.1.spectra = bf16[128,16,1024]{2,1,0:T(8,128)(2,1)S(1)} custom-call(bf16[8,16,128,128]{3,2,1,0:T(8,128)(2,1)S(1)} %copy-done.1, f32[4,128,128]{2,1,0:T(8,128)S(1)} %bitcast.6, bf16[256,128]{1,0:T(8,128)(2,1)S(1)} %copy-done.6, f32[128,128]{1,0:T(8,128)S(1)} %copy-done.5, f32[128,128]{1,0:T(8,128)S(1)} %copy-done.4, ...), custom_call_target="tpu_custom_call" | custom-call | tf_op jit(solution)/shard_map/channelise/pallas_call | solution.py:218
  104.8 0.0 copy-start.2
  104.8 2.0 copy-done.2
  106.8 93.2 %exchange.1.spectra = bf16[2048,1024]{1,0:T(8,128)(2,1)} custom-call(bf16[128,16,1024]{2,1,0:T(8,128)(2,1)} %copy-done.2), custom_call_target="tpu_custom_call" | custom-call | tf_op jit(solution)/shard_map/exchange/pallas_call | solution.py:228
  200.0 0.0 copy-start
  200.1 2.2 copy-done
  202.2 26.4 %correlate.1 = bf16[1,2048,2048]{2,1,0:T(8,128)(2,1)} custom-call(bf16[2048,1024]{1,0:T(8,128)(2,1)S(1)} %copy-done), custom_call_target="tpu_custom_call" | custom-call | tf_op jit(solution)/shard_map/correlate/pallas_call | solution.py:240
Async XLA Ops:
  8.6 74.4 %copy-start.3 = (bf16[128,256]{1,0:T(8,128)(2,1)S(1)}, bf16[128,256]{1,0:T(8,128)(2,1)}, u32[]{:S(2)}) copy-start(bf16[128,256]{1,0:T(8,128)(2,1)} %constant.58.clone.second) | copy-start | bytes 196612
  8.6 74.4 %copy-start.4 = (f32[128,128]{1,0:T(8,128)S(1)}, f32[128,128]{1,0:T(8,128)}, u32[]{:S(2)}) copy-start(f32[128,128]{1,0:T(8,128)} %constant.57.clone.twist_sin) | copy-start | bytes 196612
  8.6 74.4 %copy-start.5 = (f32[128,128]{1,0:T(8,128)S(1)}, f32[128,128]{1,0:T(8,128)}, u32[]{:S(2)}) copy-start(f32[128,128]{1,0:T(8,128)} %constant.56.clone.twist_cos) | copy-start | bytes 196612
  8.6 74.4 %copy-start.6 = (bf16[256,128]{1,0:T(8,128)(2,1)S(1)}, bf16[256,128]{1,0:T(8,128)(2,1)}, u32[]{:S(2)}) copy-start(bf16[256,128]{1,0:T(8,128)(2,1)} %constant.55.clone.first) | copy-start | bytes 196612
  83.0 2.2 copy-start.1
  104.8 2.0 copy-start.2
  200.0 2.2 copy-start

commit v2 on v1

v2 whole, which is shorter than its diff:
```python
import functools

import jax
import jax.numpy as jnp
import numpy as np
from jax import lax
from jax.experimental import pallas as pl
from jax.experimental.pallas import tpu as pltpu
from jax.sharding import PartitionSpec as P

R = 128
HALF = R // 2
N_TIME = 8
N_CHAN = 16
MESH = pl.DeviceIdType.MESH
two_pi = 2.0 * np.pi


def dft_tables():
    indices = np.arange(R)
    outer = indices[:, None] * indices[None, :]
    angles = two_pi / R * (outer % R)
    cos, sin = np.cos(angles), np.sin(angles)
    first = np.concatenate([cos, -sin], axis=0)
    twist = two_pi / (R * R) * outer
    cos_m, sin_m = cos[:HALF], sin[:HALF]
    second = np.concatenate(
        [np.concatenate([cos_m, sin_m], axis=1), np.concatenate([-sin_m, cos_m], axis=1)], axis=0
    )
    return (
        jnp.asarray(first, jnp.bfloat16),
        jnp.asarray(np.stack([np.cos(twist), np.sin(twist)]), jnp.float32),
        jnp.asarray(second, jnp.bfloat16),
    )


def place():
    tm, chan = lax.axis_index("tm"), lax.axis_index("chan")
    return 2 * (tm // 4) + chan // 2 % 2, tm % 4, chan // 4, chan % 2


def channel_kernel(
    volts, delays_in, dead_in, taps_in, first_in, twist_in, second_in,
    out,
    delays, dead_inputs, raw_taps, first, twist, second,
    own, wide, blocks, times, taps, rot, turned_rows, spectra,
    table_sem, load_sem, send_times, recv_times, send_spectra, recv_spectra,
):
    share = times.shape[1]
    n_taps = raw_taps.shape[0]
    pieces = recv_times.shape[0]
    per = share // pieces
    groups = spectra.shape[0]
    tm, chan = lax.axis_index("tm"), lax.axis_index("chan")

    def partner(step):
        along_y = (3 * step) % 4
        across = step % 2 * (1 - step // 4) + (1 - step % 2) * (step // 4)
        return (tm // 4 + across) % 2 * 4 + (tm + along_y) % 4

    def rows_of(owner):
        return pl.ds(pl.multiple_of(owner * share, share), share)

    def load(step):
        rows = rows_of(partner(step % N_TIME))
        return pltpu.make_async_copy(volts.at[rows], own.at[rows], load_sem.at[step % N_TIME])

    def start_load(step, carry):
        load(step).start()
        return carry

    def spread(owner, target):
        rows = rows_of(owner)
        for a in range(R):
            wide[a * share : (a + 1) * share, :] = own[rows, a * R : (a + 1) * R].astype(jnp.float32)
        for s in range(share):
            target[s] = wide[pl.ds(s, R, stride=share), :].astype(jnp.bfloat16)

    def send_piece(step, piece):
        owner = partner(step)
        some = pl.ds(piece * per, per)
        pltpu.make_async_remote_copy(
            src_ref=blocks.at[owner, some],
            dst_ref=times.at[tm, some],
            send_sem=send_times,
            recv_sem=recv_times.at[piece],
            device_id={"tm": owner},
            device_id_type=MESH,
        ).start()

    def first_piece(step, carry):
        owner = partner(step)
        load(step).wait()
        spread(owner, blocks.at[owner])
        send_piece(step, 0)
        return carry

    lax.fori_loop(1, N_TIME + 1, start_load, 0)
    sources = (delays_in, dead_in, taps_in, first_in, twist_in, second_in)
    places = (delays, dead_inputs, raw_taps, first, twist, second)
    tables = [
        pltpu.make_async_copy(source, place, table_sem.at[index])
        for index, (source, place) in enumerate(zip(sources, places))
    ]
    for table in tables:
        table.start()
    lax.fori_loop(1, N_TIME, first_piece, 0)

    def later_piece(index, carry):
        send_piece(index % (N_TIME - 1) + 1, index // (N_TIME - 1) + 1)
        return carry

    lax.fori_loop(0, (N_TIME - 1) * (pieces - 1), later_piece, 0)
    load(0).wait()
    spread(tm, times.at[tm])

    for table in tables:
        table.wait()
    for a in range(R):
        taps[pl.ds(a, n_taps, stride=R), :] = raw_taps[:, a * R : (a + 1) * R]
    channels = lax.broadcasted_iota(jnp.int32, (HALF, R), 0) * R + lax.broadcasted_iota(
        jnp.int32, (HALF, R), 1
    )

    def one_rotation(s, carry):
        phases = (two_pi / (R * R)) * (channels * delays[tm * share + s] & (R * R - 1)).astype(jnp.float32)
        weight = (1 - dead_inputs[tm * share + s]).astype(jnp.float32) / R
        rot[0, s] = jnp.cos(phases) * weight
        rot[1, s] = jnp.sin(phases) * weight
        return carry

    lax.fori_loop(0, share, one_rotation, 0)

    low = lax.broadcasted_iota(jnp.int32, (HALF, R), 1) < HALF

    def one_signal(s, carry):
        spectrum = [None] * N_TIME
        for t in range(N_TIME):
            filtered = taps[:R] * times[t, s].astype(jnp.float32)
            for j in range(1, min(n_taps, t + 1)):
                filtered = filtered + taps[j * R : (j + 1) * R] * times[t - j, s].astype(jnp.float32)
            sums = jnp.dot(
                first[...], filtered.astype(jnp.bfloat16), preferred_element_type=jnp.float32
            )
            real, imag = sums[:R], sums[R:]
            turned = jnp.concatenate(
                [
                    (real * twist[0] + imag * twist[1]).astype(jnp.bfloat16),
                    (imag * twist[0] - real * twist[1]).astype(jnp.bfloat16),
                ],
                axis=1,
            )
            raw = lax.dot_general(
                second[...],
                turned,
                (((1,), (1,)), ((), ())),
                preferred_element_type=jnp.float32,
            )
            rot_cos, rot_sin = rot[0, s], rot[1, s]
            spectrum[t] = (
                raw[:HALF] * rot_cos - raw[HALF:] * rot_sin,
                raw[:HALF] * rot_sin + raw[HALF:] * rot_cos,
            )
            if t % 2 == 1:
                for part in range(2):
                    even, odd = spectrum[t - 1][part], spectrum[t][part]
                    lower = jnp.where(low, even, pltpu.roll(odd, HALF, 1))
                    upper = jnp.where(low, pltpu.roll(even, HALF, 1), odd)
                    tile = (t // 2) * 2 + part
                    for half, value in enumerate((lower, upper)):
                        row = ((tile * 2 + half) * share + s) * HALF
                        turned_rows[pl.ds(pl.multiple_of(row, HALF), HALF), :] = value
        return carry

    def one_piece(piece, carry):
        arrived = times.at[pl.ds(0, N_TIME - 1), pl.ds(piece * per, per)]
        pltpu.make_async_copy(arrived, arrived, recv_times.at[piece]).wait()
        lax.fori_loop(piece * per, (piece + 1) * per, one_signal, 0)
        return carry

    lax.fori_loop(0, pieces, one_piece, 0)

    here = pl.ds(pl.multiple_of((chan * N_TIME + tm) * share, share), share)
    x, y, z, core = place()

    def owner_of(step):
        to_x = (x + step // 16 + step) % 4
        to_y = (y + step) % 4
        to_z = (z + step // 4 + step) % 4
        return to_x // 2 * 4 + to_y, to_z * 2 + to_x % 2

    def gather_rows(m, half):
        for tile in range(N_TIME):
            base = (tile * 2 + half) * share * HALF
            rows = turned_rows[pl.ds(base + m, share, stride=HALF), :]
            spectra[2 * m + half, :, tile * R : (tile + 1) * R] = rows.astype(jnp.bfloat16)

    def send_half(step, half):
        to_tm, to_pair = owner_of(step)
        pltpu.make_async_remote_copy(
            src_ref=spectra.at[(to_tm * 8 + to_pair) * 2 + half],
            dst_ref=out.at[here],
            send_sem=send_spectra,
            recv_sem=recv_spectra,
            device_id={"tm": to_tm, "chan": to_pair * 2 + half},
            device_id_type=MESH,
        ).start()

    def one_chip(step, carry):
        to_tm, to_pair = owner_of(step)
        for half in range(2):
            gather_rows(to_tm * 8 + to_pair, half)
        for half in range(2):
            send_half(step, half)
        return carry

    lax.fori_loop(1, groups // 2, one_chip, 0)
    for half in range(2):
        gather_rows(tm * 8 + chan // 2, half)
    send_half(0, 1 - core)
    pltpu.make_async_copy(spectra.at[tm * N_CHAN + chan], out.at[here], recv_spectra).start()

    sent = blocks.at[pl.ds(0, N_TIME - 1)]
    pltpu.make_async_copy(sent, sent, send_times).wait()
    sent = spectra.at[pl.ds(0, groups - 1)]
    pltpu.make_async_copy(sent, sent, send_spectra).wait()
    pltpu.make_async_copy(out, out, recv_spectra).wait()


def correlate_kernel(scale, spectra, out, left, right):
    signals, depth = left.shape
    block = out.shape[1]
    tall = 2 * block
    j = pl.program_id(0)

    @pl.when(j == 0)
    def _():
        left[...] = spectra[...]
        for b in range(signals // block):
            right[b] = spectra[b * block : (b + 1) * block, :].T

    def product(rows):
        sums = jnp.dot(left[rows, :], right[j], preferred_element_type=jnp.float32)
        return (sums * scale).astype(out.dtype)

    for m in range(signals // tall):
        rows = slice(m * tall, (m + 1) * tall)
        out[rows, :] = product(rows)
    here = pl.ds(pl.multiple_of(j * block, block), block)
    own = left[here, :]
    for pair in range(depth // (2 * R)):
        real = slice(2 * pair * R, (2 * pair + 1) * R)
        imag = slice((2 * pair + 1) * R, (2 * pair + 2) * R)
        left[here, real] = own[:, imag]
        left[here, imag] = -own[:, real]
    shape = (block, block)
    lower = lax.broadcasted_iota(jnp.int32, shape, 0) >= lax.broadcasted_iota(jnp.int32, shape, 1)
    out[here, :] = jnp.where(lower, out[here, :], product(here))


def shards(voltages, filter_taps, delays, dead_inputs):
    signals_here = voltages.shape[0]
    share = signals_here // N_TIME
    signals = signals_here * N_CHAN
    groups = N_TIME * N_CHAN
    depth = N_TIME * R
    in_hbm = pl.BlockSpec(memory_space=pltpu.HBM)
    pieces = 8
    tables = dft_tables()

    everyone = pl.pallas_call(
        channel_kernel,
        out_shape=jax.ShapeDtypeStruct((signals, depth), jnp.bfloat16),
        in_specs=[in_hbm] * 7,
        out_specs=in_hbm,
        scratch_shapes=[
            pltpu.SMEM(delays.shape, jnp.int32),
            pltpu.SMEM(dead_inputs.shape, jnp.int32),
            pltpu.VMEM(filter_taps.shape, jnp.float32),
            *(pltpu.VMEM(table.shape, table.dtype) for table in tables),
            pltpu.VMEM(voltages.shape, jnp.bfloat16),
            pltpu.VMEM((R * share, R), jnp.float32),
            pltpu.VMEM((N_TIME, share, R, R), jnp.bfloat16),
            pltpu.VMEM((N_TIME, share, R, R), jnp.bfloat16),
            pltpu.VMEM((filter_taps.shape[0] * R, R), jnp.float32),
            pltpu.VMEM((2, share, HALF, R), jnp.float32),
            pltpu.VMEM((N_TIME * 2 * share * HALF, R), jnp.float32),
            pltpu.VMEM((groups, share, depth), jnp.bfloat16),
            pltpu.SemaphoreType.DMA((3 + len(tables),)),
            pltpu.SemaphoreType.DMA((N_TIME,)),
            pltpu.SemaphoreType.DMA,
            pltpu.SemaphoreType.DMA((pieces,)),
            pltpu.SemaphoreType.DMA,
            pltpu.SemaphoreType.DMA,
        ],
        compiler_params=pltpu.CompilerParams(has_side_effects=True, vmem_limit_bytes=48 * 2**20),
        name="channels",
    )(voltages, delays, dead_inputs, filter_taps, *tables)

    block = 256
    scale = 1.0 / (HALF * N_TIME)
    return pl.pallas_call(
        functools.partial(correlate_kernel, scale),
        grid=(signals // block,),
        out_shape=jax.ShapeDtypeStruct((1, signals, signals), jnp.bfloat16),
        in_specs=[pl.BlockSpec((signals, depth), lambda j: (0, 0), pipeline_mode=pl.Buffered(1))],
        out_specs=pl.BlockSpec((None, signals, block), lambda j: (0, 0, j)),
        scratch_shapes=[
            pltpu.VMEM((signals, depth), jnp.bfloat16),
            pltpu.VMEM((signals // block, depth, block), jnp.bfloat16),
        ],
        compiler_params=pltpu.CompilerParams(vmem_limit_bytes=40 * 2**20),
        name="correlate",
    )(everyone)


def solution(mesh):
    in_specs = (P("chan", "tm"), P(), P("chan"), P("chan"))
    out_specs = P(("tm", "chan"), None, None)
    return jax.shard_map(shards, mesh=mesh, in_specs=in_specs, out_specs=out_specs, check_vma=False)
```

time: 229 us -> 139 us (0.61)
  the two profiles are of different devices: /device:TPU:29 before, /device:TPU:1 now
where the time goes in v2:
time: 139 us; the launch traced here: 138 us
  Pallas kernels  133 us (96%)
  local copies, waits for them, and re-layouts  4.84 us (3%)
    pallas_call x1, Pallas kernels, shards(): pl.pallas_call(channel_kernel, out_shape=jax.ShapeDtypeStruct((signals, d...  119 us
    pallas_call x1, Pallas kernels, shards(): pl.pallas_call(functools.partial(correlate_kernel, scale), grid=(signals...  13.8 us
    unnamed x12, local copies, waits for them, and re-layouts  4.84 us

profile of v2, /device:TPU:1, one launch (start us, length us, event | category | flops | bytes accessed | tf_op | source)
XLA Modules:
  0.0 137.8 jit_solution(15365489487886714663)
XLA Ops:
  0.0 0.0 copy-start
  0.0 0.9 copy-done
  1.0 0.0 copy-start.1
  1.0 0.9 copy-done.1
  1.9 0.0 copy-start.2
  1.9 0.8 copy-done.2
  2.7 0.0 copy-start.3
  2.7 0.8 copy-done.3
  3.5 0.0 copy-start.4
  3.5 0.7 copy-done.4
  4.2 0.0 copy-start.5
  4.2 0.7 copy-done.5
  4.8 119.2 %channels.1.spectra = bf16[2048,1024]{1,0:T(8,128)(2,1)S(1)} custom-call(bf16[128,16384]{1,0:T(8,128)(2,1)} %volts.1, s32[128]{0:T(128)S(1)} %copy-done.4, s32[128]{0:T(128)S(1)} %copy-done.5, f32[4,16384]{1,0:T(4,128)S(1)} %copy-done, bf16[256,128]{1,0:T(8,128)(2,1)S(1)} %copy-done.3, f32[2,128,128]{2,1,0:T(8,128)S(1)} %copy-done.1, ...), custom_call_target="tpu_custom_call" | custom-call | tf_op jit(solution)/shard_map/channels/pallas_call | solution.py:271
  124.1 13.8 %correlate.1 = bf16[1,2048,2048]{2,1,0:T(8,128)(2,1)} custom-call(bf16[2048,1024]{1,0:T(8,128)(2,1)S(1)} %channels.1.spectra), custom_call_target="tpu_custom_call" | custom-call | tf_op jit(solution)/shard_map/correlate/pallas_call | solution.py:302
Async XLA Ops:
  0.0 0.9 copy-start
  1.0 0.9 copy-start.1
  1.9 0.8 copy-start.2
  2.7 0.8 copy-start.3
  3.5 0.7 copy-start.4
  4.2 0.7 copy-start.5

commit v3 on v2

--- a/solution.py
+++ b/solution.py
@@ -12,6 +12,8 @@
 HALF = R // 2
 N_TIME = 8
 N_CHAN = 16
+VMEM_LIMIT = 60 * 2**20
+EARLY, LATE = 4, 4
 MESH = pl.DeviceIdType.MESH
 two_pi = 2.0 * np.pi
 
@@ -40,17 +42,19 @@
 
 
 def channel_kernel(
+    scale,
     volts, delays_in, dead_in, taps_in, first_in, twist_in, second_in,
-    out,
+    late, early_sums,
     delays, dead_inputs, raw_taps, first, twist, second,
-    own, wide, blocks, times, taps, rot, turned_rows, spectra,
-    table_sem, load_sem, send_times, recv_times, send_spectra, recv_spectra,
+    own, wide, blocks, times, taps, rot, turned_rows, early_spectra, late_spectra,
+    early, right, sums_out,
+    table_sem, load_sem, send_times, recv_times, send_spectra, recv_early, recv_late, sums_sem,
 ):
     share = times.shape[1]
     n_taps = raw_taps.shape[0]
     pieces = recv_times.shape[0]
     per = share // pieces
-    groups = spectra.shape[0]
+    groups = early_spectra.shape[0]
     tm, chan = lax.axis_index("tm"), lax.axis_index("chan")
 
     def partner(step):
@@ -189,64 +193,90 @@
         to_z = (z + step // 4 + step) % 4
         return to_x // 2 * 4 + to_y, to_z * 2 + to_x % 2
 
-    def gather_rows(m, half):
-        for tile in range(N_TIME):
-            base = (tile * 2 + half) * share * HALF
+    sources = (early_spectra, late_spectra)
+
+    def gather_rows(m, half, part):
+        for index in range((EARLY, LATE)[part]):
+            base = ((part * EARLY + index) * 2 + half) * share * HALF
             rows = turned_rows[pl.ds(base + m, share, stride=HALF), :]
-            spectra[2 * m + half, :, tile * R : (tile + 1) * R] = rows.astype(jnp.bfloat16)
-
-    def send_half(step, half):
+            sources[part][2 * m + half, :, index * R : (index + 1) * R] = rows.astype(jnp.bfloat16)
+
+    def send_half(step, half, part):
         to_tm, to_pair = owner_of(step)
         pltpu.make_async_remote_copy(
-            src_ref=spectra.at[(to_tm * 8 + to_pair) * 2 + half],
-            dst_ref=out.at[here],
-            send_sem=send_spectra,
-            recv_sem=recv_spectra,
+            src_ref=sources[part].at[(to_tm * 8 + to_pair) * 2 + half],
+            dst_ref=(early, late)[part].at[here],
+            send_sem=send_spectra.at[part],
+            recv_sem=(recv_early, recv_late)[part],
             device_id={"tm": to_tm, "chan": to_pair * 2 + half},
             device_id_type=MESH,
         ).start()
 
-    def one_chip(step, carry):
-        to_tm, to_pair = owner_of(step)
+    for part in range(2):
+
+        def one_chip(step, carry):
+            to_tm, to_pair = owner_of(step)
+            for half in range(2):
+                gather_rows(to_tm * 8 + to_pair, half, part)
+            for half in range(2):
+                send_half(step, half, part)
+            return carry
+
+        lax.fori_loop(1, groups // 2, one_chip, 0)
         for half in range(2):
-            gather_rows(to_tm * 8 + to_pair, half)
-        for half in range(2):
-            send_half(step, half)
-        return carry
-
-    lax.fori_loop(1, groups // 2, one_chip, 0)
-    for half in range(2):
-        gather_rows(tm * 8 + chan // 2, half)
-    send_half(0, 1 - core)
-    pltpu.make_async_copy(spectra.at[tm * N_CHAN + chan], out.at[here], recv_spectra).start()
+            gather_rows(tm * 8 + chan // 2, half, part)
+        send_half(0, 1 - core, part)
+        pltpu.make_async_copy(
+            sources[part].at[tm * N_CHAN + chan], (early, late)[part].at[here], (recv_early, recv_late)[part]
+        ).start()
+
+    pltpu.make_async_copy(early, early, recv_early).wait()
+    block = right.shape[1]
+
+    def sums_copy(j):
+        columns = pl.ds(pl.multiple_of(j * block, block), block)
+        return pltpu.make_async_copy(sums_out.at[j % 2], early_sums.at[:, columns], sums_sem.at[j % 2])
+
+    def column(j, carry):
+        @pl.when(j >= 2)
+        def _():
+            sums_copy(j - 2).wait()
+
+        def emit(rows, sums, lower):
+            total = (sums * scale).astype(jnp.bfloat16)
+            slot = sums_out.at[j % 2]
+            slot[rows, :] = total if lower is None else jnp.where(lower, slot[rows, :], total)
+
+        column_block(early, right, j, emit)
+        sums_copy(j).start()
+        return carry
+
+    columns = early_sums.shape[1] // block
+    lax.fori_loop(0, columns, column, 0)
+    sums_copy(columns - 2).wait()
+    sums_copy(columns - 1).wait()
 
     sent = blocks.at[pl.ds(0, N_TIME - 1)]
     pltpu.make_async_copy(sent, sent, send_times).wait()
-    sent = spectra.at[pl.ds(0, groups - 1)]
-    pltpu.make_async_copy(sent, sent, send_spectra).wait()
-    pltpu.make_async_copy(out, out, recv_spectra).wait()
-
-
-def correlate_kernel(scale, spectra, out, left, right):
+    for part in range(2):
+        sent = sources[part].at[pl.ds(0, groups - 1)]
+        pltpu.make_async_copy(sent, sent, send_spectra.at[part]).wait()
+    pltpu.make_async_copy(late, late, recv_late).wait()
+
+
+def column_block(left, right, j, emit):
     signals, depth = left.shape
-    block = out.shape[1]
-    tall = 2 * block
-    j = pl.program_id(0)
-
-    @pl.when(j == 0)
-    def _():
-        left[...] = spectra[...]
-        for b in range(signals // block):
-            right[b] = spectra[b * block : (b + 1) * block, :].T
+    block = right.shape[1]
+    tall = signals
+    here = pl.ds(pl.multiple_of(j * block, block), block)
+    right[...] = left[here, :].T
 
     def product(rows):
-        sums = jnp.dot(left[rows, :], right[j], preferred_element_type=jnp.float32)
-        return (sums * scale).astype(out.dtype)
+        return jnp.dot(left[rows, :], right[...], preferred_element_type=jnp.float32)
 
     for m in range(signals // tall):
-        rows = slice(m * tall, (m + 1) * tall)
-        out[rows, :] = product(rows)
-    here = pl.ds(pl.multiple_of(j * block, block), block)
+        rows = pl.ds(m * tall, tall)
+        emit(rows, product(rows), None)
     own = left[here, :]
     for pair in range(depth // (2 * R)):
         real = slice(2 * pair * R, (2 * pair + 1) * R)
@@ -255,7 +285,43 @@
         left[here, imag] = -own[:, real]
     shape = (block, block)
     lower = lax.broadcasted_iota(jnp.int32, shape, 0) >= lax.broadcasted_iota(jnp.int32, shape, 1)
-    out[here, :] = jnp.where(lower, out[here, :], product(here))
+    emit(here, product(here), lower)
+
+
+def correlate_kernel(scale, late, early_sums, out, left, right, sums_in, result, late_sem, in_sem, out_sem):
+    block = right.shape[1]
+    columns = out.shape[2] // block
+
+    def columns_of(j):
+        return pl.ds(pl.multiple_of(j * block, block), block)
+
+    def load(j):
+        return pltpu.make_async_copy(early_sums.at[:, columns_of(j)], sums_in.at[j], in_sem.at[j])
+
+    def store(j):
+        return pltpu.make_async_copy(result.at[j], out.at[0, :, columns_of(j)], out_sem.at[j])
+
+    load_left = pltpu.make_async_copy(late, left, late_sem)
+    load_left.start()
+    for j in range(columns):
+        load(j).start()
+    load_left.wait()
+
+    def column(j, carry):
+        load(j).wait()
+        earlier, total = sums_in.at[j], result.at[j]
+
+        def emit(rows, sums, lower):
+            values = (sums * scale + earlier[rows, :].astype(jnp.float32)).astype(out.dtype)
+            total[rows, :] = values if lower is None else jnp.where(lower, total[rows, :], values)
+
+        column_block(left, right, j, emit)
+        store(j).start()
+        return carry
+
+    lax.fori_loop(0, columns, column, 0)
+    for j in range(columns):
+        store(j).wait()
 
 
 def shards(voltages, filter_taps, delays, dead_inputs):
@@ -263,16 +329,20 @@
     share = signals_here // N_TIME
     signals = signals_here * N_CHAN
     groups = N_TIME * N_CHAN
-    depth = N_TIME * R
     in_hbm = pl.BlockSpec(memory_space=pltpu.HBM)
-    pieces = 8
+    pieces = 16
+    block, last_block = 512, 512
+    scale = 1.0 / (HALF * N_TIME)
     tables = dft_tables()
 
-    everyone = pl.pallas_call(
-        channel_kernel,
-        out_shape=jax.ShapeDtypeStruct((signals, depth), jnp.bfloat16),
+    late, early_sums = pl.pallas_call(
+        functools.partial(channel_kernel, scale),
+        out_shape=[
+            jax.ShapeDtypeStruct((signals, LATE * R), jnp.bfloat16),
+            jax.ShapeDtypeStruct((signals, signals), jnp.bfloat16),
+        ],
         in_specs=[in_hbm] * 7,
-        out_specs=in_hbm,
+        out_specs=[in_hbm, in_hbm],
         scratch_shapes=[
             pltpu.SMEM(delays.shape, jnp.int32),
             pltpu.SMEM(dead_inputs.shape, jnp.int32),
@@ -285,33 +355,41 @@
             pltpu.VMEM((filter_taps.shape[0] * R, R), jnp.float32),
             pltpu.VMEM((2, share, HALF, R), jnp.float32),
             pltpu.VMEM((N_TIME * 2 * share * HALF, R), jnp.float32),
-            pltpu.VMEM((groups, share, depth), jnp.bfloat16),
+            pltpu.VMEM((groups, share, EARLY * R), jnp.bfloat16),
+            pltpu.VMEM((groups, share, LATE * R), jnp.bfloat16),
+            pltpu.VMEM((signals, EARLY * R), jnp.bfloat16),
+            pltpu.VMEM((EARLY * R, block), jnp.bfloat16),
+            pltpu.VMEM((2, signals, block), jnp.bfloat16),
             pltpu.SemaphoreType.DMA((3 + len(tables),)),
             pltpu.SemaphoreType.DMA((N_TIME,)),
             pltpu.SemaphoreType.DMA,
             pltpu.SemaphoreType.DMA((pieces,)),
+            pltpu.SemaphoreType.DMA((2,)),
             pltpu.SemaphoreType.DMA,
             pltpu.SemaphoreType.DMA,
+            pltpu.SemaphoreType.DMA((2,)),
         ],
-        compiler_params=pltpu.CompilerParams(has_side_effects=True, vmem_limit_bytes=48 * 2**20),
+        compiler_params=pltpu.CompilerParams(has_side_effects=True, vmem_limit_bytes=VMEM_LIMIT),
         name="channels",
     )(voltages, delays, dead_inputs, filter_taps, *tables)
 
-    block = 256
-    scale = 1.0 / (HALF * N_TIME)
     return pl.pallas_call(
         functools.partial(correlate_kernel, scale),
-        grid=(signals // block,),
         out_shape=jax.ShapeDtypeStruct((1, signals, signals), jnp.bfloat16),
-        in_specs=[pl.BlockSpec((signals, depth), lambda j: (0, 0), pipeline_mode=pl.Buffered(1))],
-        out_specs=pl.BlockSpec((None, signals, block), lambda j: (0, 0, j)),
+        in_specs=[in_hbm, in_hbm],
+        out_specs=in_hbm,
         scratch_shapes=[
-            pltpu.VMEM((signals, depth), jnp.bfloat16),
-            pltpu.VMEM((signals // block, depth, block), jnp.bfloat16),
+            pltpu.VMEM((signals, LATE * R), jnp.bfloat16),
+            pltpu.VMEM((LATE * R, last_block), jnp.bfloat16),
+            pltpu.VMEM((signals // last_block, signals, last_block), jnp.bfloat16),
+            pltpu.VMEM((signals // last_block, signals, last_block), jnp.bfloat16),
+            pltpu.SemaphoreType.DMA,
+            pltpu.SemaphoreType.DMA((signals // last_block,)),
+            pltpu.SemaphoreType.DMA((signals // last_block,)),
         ],
-        compiler_params=pltpu.CompilerParams(vmem_limit_bytes=40 * 2**20),
+        compiler_params=pltpu.CompilerParams(vmem_limit_bytes=VMEM_LIMIT),
         name="correlate",
-    )(everyone)
+    )(late, early_sums)
 
 
 def solution(mesh):

time: 139 us -> 127 us (0.914)
  Pallas kernels: 133 us -> 127 us
  local copies, waits for them, and re-layouts: 4.84 us -> 0 us
    pallas_call x2, Pallas kernels: 133 us -> 127 us  [the longest x1 115 us: shards(): pl.pallas_call(functools.partial(channel_kernel, scale), out_shape=[jax.S...]
    unnamed x12 -> x0, local copies, waits for them, and re-layouts: 4.84 us -> none
where the time goes in v3:
time: 127 us
  Pallas kernels  127 us (100%)
    pallas_call x1, Pallas kernels, shards(): pl.pallas_call(functools.partial(channel_kernel, scale), out_shape=[jax.S...  115 us
    pallas_call x1, Pallas kernels, shards(): pl.pallas_call(functools.partial(correlate_kernel, scale), out_shape=jax....  11.8 us

profile of v3, /device:TPU:1, one launch (start us, length us, event | category | flops | bytes accessed | tf_op | source)
XLA Modules:
  0.0 127.0 jit_solution(8357480846021722539)
XLA Ops:
  0.0 115.2 %channels.1 = (bf16[2048,512]{1,0:T(8,128)(2,1)}, bf16[2048,2048]{1,0:T(8,128)(2,1)}) custom-call(bf16[128,16384]{1,0:T(8,128)(2,1)} %volts.1, s32[128]{0:T(128)} %delays_in.1, s32[128]{0:T(128)} %dead_in.1, f32[4,16384]{1,0:T(4,128)} %taps_in.1, bf16[256,128]{1,0:T(8,128)(2,1)} %constant.6.clone.first_in, f32[2,128,128]{2,1,0:T(8,128)} %constant.7.clone.twist_in, ...), custom_call_target="tpu_custom_call" | custom-call | tf_op jit(solution)/shard_map/channels/pallas_call | solution.py:338
  115.2 11.8 %correlate.1 = bf16[1,2048,2048]{2,1,0:T(8,128)(2,1)} custom-call(bf16[2048,512]{1,0:T(8,128)(2,1)} %get-tuple-element.7.late, bf16[2048,2048]{1,0:T(8,128)(2,1)} %get-tuple-element.8.early_sums), custom_call_target="tpu_custom_call" | custom-call | tf_op jit(solution)/shard_map/correlate/pallas_call | solution.py:376

commit v4 on v3

--- a/solution.py
+++ b/solution.py
@@ -13,7 +13,7 @@
 N_TIME = 8
 N_CHAN = 16
 VMEM_LIMIT = 60 * 2**20
-EARLY, LATE = 4, 4
+PARTS = (4, 2, 2)
 MESH = pl.DeviceIdType.MESH
 two_pi = 2.0 * np.pi
 
@@ -46,16 +46,29 @@
     volts, delays_in, dead_in, taps_in, first_in, twist_in, second_in,
     late, early_sums,
     delays, dead_inputs, raw_taps, first, twist, second,
-    own, wide, blocks, times, taps, rot, turned_rows, early_spectra, late_spectra,
-    early, right, sums_out,
-    table_sem, load_sem, send_times, recv_times, send_spectra, recv_early, recv_late, sums_sem,
+    own, wide, blocks, times, taps, rot, turned_rows, outgoing,
+    earlies, rights, early_total, sums_out,
+    table_sem, load_sem, send_times, recv_times, send_spectra, recv_spectra, sums_sem, everyone_in,
 ):
     share = times.shape[1]
     n_taps = raw_taps.shape[0]
     pieces = recv_times.shape[0]
     per = share // pieces
-    groups = early_spectra.shape[0]
+    groups = outgoing[0].shape[0]
     tm, chan = lax.axis_index("tm"), lax.axis_index("chan")
+
+    barrier = pltpu.get_barrier_semaphore()
+
+    def greet(sem, axis, size):
+        def one(step, carry):
+            other = lax.rem(lax.axis_index(axis) + step, size)
+            pl.semaphore_signal(sem, inc=1, device_id={axis: other}, device_id_type=MESH)
+            return carry
+
+        lax.fori_loop(1, size, one, 0)
+
+    greet(barrier, "tm", N_TIME)
+    greet(barrier, "chan", N_CHAN)
 
     def partner(step):
         along_y = (3 * step) % 4
@@ -96,6 +109,12 @@
         owner = partner(step)
         load(step).wait()
         spread(owner, blocks.at[owner])
+
+        @pl.when(step == 1)
+        def _():
+            pl.semaphore_wait(barrier, N_TIME - 1 + N_CHAN - 1)
+            greet(everyone_in, "tm", N_TIME)
+
         send_piece(step, 0)
         return carry
 
@@ -193,26 +212,27 @@
         to_z = (z + step // 4 + step) % 4
         return to_x // 2 * 4 + to_y, to_z * 2 + to_x % 2
 
-    sources = (early_spectra, late_spectra)
+    received = (*earlies, late)
 
     def gather_rows(m, half, part):
-        for index in range((EARLY, LATE)[part]):
-            base = ((part * EARLY + index) * 2 + half) * share * HALF
+        for index in range(PARTS[part]):
+            base = ((sum(PARTS[:part]) + index) * 2 + half) * share * HALF
             rows = turned_rows[pl.ds(base + m, share, stride=HALF), :]
-            sources[part][2 * m + half, :, index * R : (index + 1) * R] = rows.astype(jnp.bfloat16)
+            outgoing[part][2 * m + half, :, index * R : (index + 1) * R] = rows.astype(jnp.bfloat16)
 
     def send_half(step, half, part):
         to_tm, to_pair = owner_of(step)
         pltpu.make_async_remote_copy(
-            src_ref=sources[part].at[(to_tm * 8 + to_pair) * 2 + half],
-            dst_ref=(early, late)[part].at[here],
+            src_ref=outgoing[part].at[(to_tm * 8 + to_pair) * 2 + half],
+            dst_ref=received[part].at[here],
             send_sem=send_spectra.at[part],
-            recv_sem=(recv_early, recv_late)[part],
+            recv_sem=recv_spectra.at[part],
             device_id={"tm": to_tm, "chan": to_pair * 2 + half},
             device_id_type=MESH,
         ).start()
 
-    for part in range(2):
+    pl.semaphore_wait(everyone_in, N_TIME - 1)
+    for part in range(len(PARTS)):
 
         def one_chip(step, carry):
             to_tm, to_pair = owner_of(step)
@@ -227,41 +247,55 @@
             gather_rows(tm * 8 + chan // 2, half, part)
         send_half(0, 1 - core, part)
         pltpu.make_async_copy(
-            sources[part].at[tm * N_CHAN + chan], (early, late)[part].at[here], (recv_early, recv_late)[part]
+            outgoing[part].at[tm * N_CHAN + chan], received[part].at[here], recv_spectra.at[part]
         ).start()
 
-    pltpu.make_async_copy(early, early, recv_early).wait()
-    block = right.shape[1]
+    def arrive(part):
+        pltpu.make_async_copy(received[part], received[part], recv_spectra.at[part]).wait()
+
+    block = sums_out.shape[2]
+    columns = early_sums.shape[1] // block
+
+    def first_column(j, carry):
+        total = early_total.at[j]
+
+        def emit(rows, sums, lower):
+            total[rows, :] = sums if lower is None else jnp.where(lower, total[rows, :], sums)
+
+        column_block(earlies[0], rights[0], j, emit)
+        return carry
 
     def sums_copy(j):
-        columns = pl.ds(pl.multiple_of(j * block, block), block)
-        return pltpu.make_async_copy(sums_out.at[j % 2], early_sums.at[:, columns], sums_sem.at[j % 2])
-
-    def column(j, carry):
+        some = pl.ds(pl.multiple_of(j * block, block), block)
+        return pltpu.make_async_copy(sums_out.at[j % 2], early_sums.at[:, some], sums_sem.at[j % 2])
+
+    def second_column(j, carry):
         @pl.when(j >= 2)
         def _():
             sums_copy(j - 2).wait()
 
         def emit(rows, sums, lower):
-            total = (sums * scale).astype(jnp.bfloat16)
             slot = sums_out.at[j % 2]
+            total = ((early_total[j, rows, :] + sums) * scale).astype(jnp.bfloat16)
             slot[rows, :] = total if lower is None else jnp.where(lower, slot[rows, :], total)
 
-        column_block(early, right, j, emit)
+        column_block(earlies[1], rights[1], j, emit)
         sums_copy(j).start()
         return carry
 
-    columns = early_sums.shape[1] // block
-    lax.fori_loop(0, columns, column, 0)
+    arrive(0)
+    lax.fori_loop(0, columns, first_column, 0)
+    arrive(1)
+    lax.fori_loop(0, columns, second_column, 0)
     sums_copy(columns - 2).wait()
     sums_copy(columns - 1).wait()
 
     sent = blocks.at[pl.ds(0, N_TIME - 1)]
     pltpu.make_async_copy(sent, sent, send_times).wait()
-    for part in range(2):
-        sent = sources[part].at[pl.ds(0, groups - 1)]
+    for part in range(len(PARTS)):
+        sent = outgoing[part].at[pl.ds(0, groups - 1)]
         pltpu.make_async_copy(sent, sent, send_spectra.at[part]).wait()
-    pltpu.make_async_copy(late, late, recv_late).wait()
+    arrive(len(PARTS) - 1)
 
 
 def column_block(left, right, j, emit):
@@ -338,7 +372,7 @@
     late, early_sums = pl.pallas_call(
         functools.partial(channel_kernel, scale),
         out_shape=[
-            jax.ShapeDtypeStruct((signals, LATE * R), jnp.bfloat16),
+            jax.ShapeDtypeStruct((signals, PARTS[-1] * R), jnp.bfloat16),
             jax.ShapeDtypeStruct((signals, signals), jnp.bfloat16),
         ],
         in_specs=[in_hbm] * 7,
@@ -355,21 +389,21 @@
             pltpu.VMEM((filter_taps.shape[0] * R, R), jnp.float32),
             pltpu.VMEM((2, share, HALF, R), jnp.float32),
             pltpu.VMEM((N_TIME * 2 * share * HALF, R), jnp.float32),
-            pltpu.VMEM((groups, share, EARLY * R), jnp.bfloat16),
-            pltpu.VMEM((groups, share, LATE * R), jnp.bfloat16),
-            pltpu.VMEM((signals, EARLY * R), jnp.bfloat16),
-            pltpu.VMEM((EARLY * R, block), jnp.bfloat16),
+            [pltpu.VMEM((groups, share, part * R), jnp.bfloat16) for part in PARTS],
+            [pltpu.VMEM((signals, part * R), jnp.bfloat16) for part in PARTS[:2]],
+            [pltpu.VMEM((part * R, block), jnp.bfloat16) for part in PARTS[:2]],
+            pltpu.VMEM((signals // block, signals, block), jnp.float32),
             pltpu.VMEM((2, signals, block), jnp.bfloat16),
             pltpu.SemaphoreType.DMA((3 + len(tables),)),
             pltpu.SemaphoreType.DMA((N_TIME,)),
             pltpu.SemaphoreType.DMA,
             pltpu.SemaphoreType.DMA((pieces,)),
+            pltpu.SemaphoreType.DMA((len(PARTS),)),
+            pltpu.SemaphoreType.DMA((len(PARTS),)),
             pltpu.SemaphoreType.DMA((2,)),
-            pltpu.SemaphoreType.DMA,
-            pltpu.SemaphoreType.DMA,
-            pltpu.SemaphoreType.DMA((2,)),
+            pltpu.SemaphoreType.REGULAR,
         ],
-        compiler_params=pltpu.CompilerParams(has_side_effects=True, vmem_limit_bytes=VMEM_LIMIT),
+        compiler_params=pltpu.CompilerParams(collective_id=0, has_side_effects=True, vmem_limit_bytes=VMEM_LIMIT),
         name="channels",
     )(voltages, delays, dead_inputs, filter_taps, *tables)
 
@@ -379,8 +413,8 @@
         in_specs=[in_hbm, in_hbm],
         out_specs=in_hbm,
         scratch_shapes=[
-            pltpu.VMEM((signals, LATE * R), jnp.bfloat16),
-            pltpu.VMEM((LATE * R, last_block), jnp.bfloat16),
+            pltpu.VMEM((signals, PARTS[-1] * R), jnp.bfloat16),
+            pltpu.VMEM((PARTS[-1] * R, last_block), jnp.bfloat16),
             pltpu.VMEM((signals // last_block, signals, last_block), jnp.bfloat16),
             pltpu.VMEM((signals // last_block, signals, last_block), jnp.bfloat16),
             pltpu.SemaphoreType.DMA,

time: 127 us -> 116 us (0.913)
  Pallas kernels: 127 us -> 116 us
    pallas_call x1, Pallas kernels: 115 us -> 108 us  [shards(): pl.pallas_call(functools.partial(channel_kernel, scale), out_shape=[jax.S...]
    pallas_call x1, Pallas kernels: 11.8 us -> 8.37 us  [shards(): pl.pallas_call(functools.partial(correlate_kernel, scale), out_shape=jax....]
where the time goes in v4:
time: 116 us
  Pallas kernels  116 us (100%)
    pallas_call x1, Pallas kernels, shards(): pl.pallas_call(functools.partial(channel_kernel, scale), out_shape=[jax.S...  108 us
    pallas_call x1, Pallas kernels, shards(): pl.pallas_call(functools.partial(correlate_kernel, scale), out_shape=jax....  8.37 us

profile of v4, /device:TPU:1, one launch (start us, length us, event | category | flops | bytes accessed | tf_op | source)
XLA Modules:
  0.0 116.0 jit_solution(8780567571088787668)
XLA Ops:
  0.0 107.6 %channels.1 = (bf16[2048,256]{1,0:T(8,128)(2,1)}, bf16[2048,2048]{1,0:T(8,128)(2,1)}) custom-call(bf16[128,16384]{1,0:T(8,128)(2,1)} %volts.1, s32[128]{0:T(128)} %delays_in.1, s32[128]{0:T(128)} %dead_in.1, f32[4,16384]{1,0:T(4,128)} %taps_in.1, bf16[256,128]{1,0:T(8,128)(2,1)} %constant.6.clone.first_in, f32[2,128,128]{2,1,0:T(8,128)} %constant.7.clone.twist_in, ...), custom_call_target="tpu_custom_call" | custom-call | tf_op jit(solution)/shard_map/channels/pallas_call | solution.py:372
  107.6 8.4 %correlate.1 = bf16[1,2048,2048]{2,1,0:T(8,128)(2,1)} custom-call(bf16[2048,256]{1,0:T(8,128)(2,1)} %get-tuple-element.7.late, bf16[2048,2048]{1,0:T(8,128)(2,1)} %get-tuple-element.8.early_sums), custom_call_target="tpu_custom_call" | custom-call | tf_op jit(solution)/shard_map/correlate/pallas_call | solution.py:410

commit v5 on v4

--- a/solution.py
+++ b/solution.py
@@ -13,7 +13,7 @@
 N_TIME = 8
 N_CHAN = 16
 VMEM_LIMIT = 60 * 2**20
-PARTS = (4, 2, 2)
+N_PARTS = 4
 MESH = pl.DeviceIdType.MESH
 two_pi = 2.0 * np.pi
 
@@ -47,7 +47,7 @@
     late, early_sums,
     delays, dead_inputs, raw_taps, first, twist, second,
     own, wide, blocks, times, taps, rot, turned_rows, outgoing,
-    earlies, rights, early_total, sums_out,
+    earlies, joined, rights, early_total, sums_out,
     table_sem, load_sem, send_times, recv_times, send_spectra, recv_spectra, sums_sem, everyone_in,
 ):
     share = times.shape[1]
@@ -66,9 +66,6 @@
             return carry
 
         lax.fori_loop(1, size, one, 0)
-
-    greet(barrier, "tm", N_TIME)
-    greet(barrier, "chan", N_CHAN)
 
     def partner(step):
         along_y = (3 * step) % 4
@@ -113,12 +110,13 @@
         @pl.when(step == 1)
         def _():
             pl.semaphore_wait(barrier, N_TIME - 1 + N_CHAN - 1)
-            greet(everyone_in, "tm", N_TIME)
 
         send_piece(step, 0)
         return carry
 
     lax.fori_loop(1, N_TIME + 1, start_load, 0)
+    greet(barrier, "tm", N_TIME)
+    greet(barrier, "chan", N_CHAN)
     sources = (delays_in, dead_in, taps_in, first_in, twist_in, second_in)
     places = (delays, dead_inputs, raw_taps, first, twist, second)
     tables = [
@@ -134,6 +132,8 @@
         return carry
 
     lax.fori_loop(0, (N_TIME - 1) * (pieces - 1), later_piece, 0)
+
+    greet(everyone_in, "tm", N_TIME)
     load(0).wait()
     spread(tm, times.at[tm])
 
@@ -201,8 +201,6 @@
         lax.fori_loop(piece * per, (piece + 1) * per, one_signal, 0)
         return carry
 
-    lax.fori_loop(0, pieces, one_piece, 0)
-
     here = pl.ds(pl.multiple_of((chan * N_TIME + tm) * share, share), share)
     x, y, z, core = place()
 
@@ -213,11 +211,22 @@
         return to_x // 2 * 4 + to_y, to_z * 2 + to_x % 2
 
     received = (*earlies, late)
+    few = share // 2
 
     def gather_rows(m, half, part):
-        for index in range(PARTS[part]):
-            base = ((sum(PARTS[:part]) + index) * 2 + half) * share * HALF
-            rows = turned_rows[pl.ds(base + m, share, stride=HALF), :]
+        for index in range(2):
+            if part < 2:
+                bases = [((2 * pair + index) * 2 + half) * share * HALF for pair in range(2)]
+                rows = jnp.concatenate(
+                    [
+                        turned_rows[pl.ds(base + part * few * HALF + m, few, stride=HALF), :]
+                        for base in bases
+                    ],
+                    axis=0,
+                )
+            else:
+                base = ((2 * part + index) * 2 + half) * share * HALF
+                rows = turned_rows[pl.ds(base + m, share, stride=HALF), :]
             outgoing[part][2 * m + half, :, index * R : (index + 1) * R] = rows.astype(jnp.bfloat16)
 
     def send_half(step, half, part):
@@ -231,9 +240,7 @@
             device_id_type=MESH,
         ).start()
 
-    pl.semaphore_wait(everyone_in, N_TIME - 1)
-    for part in range(len(PARTS)):
-
+    def send_part(part):
         def one_chip(step, carry):
             to_tm, to_pair = owner_of(step)
             for half in range(2):
@@ -250,6 +257,13 @@
             outgoing[part].at[tm * N_CHAN + chan], received[part].at[here], recv_spectra.at[part]
         ).start()
 
+    lax.fori_loop(0, pieces // 2, one_piece, 0)
+    pl.semaphore_wait(everyone_in, N_TIME - 1)
+    send_part(0)
+    lax.fori_loop(pieces // 2, pieces, one_piece, 0)
+    for part in range(1, N_PARTS):
+        send_part(part)
+
     def arrive(part):
         pltpu.make_async_copy(received[part], received[part], recv_spectra.at[part]).wait()
 
@@ -262,7 +276,7 @@
         def emit(rows, sums, lower):
             total[rows, :] = sums if lower is None else jnp.where(lower, total[rows, :], sums)
 
-        column_block(earlies[0], rights[0], j, emit)
+        column_block(joined, rights[0], j, emit)
         return carry
 
     def sums_copy(j):
@@ -279,23 +293,34 @@
             total = ((early_total[j, rows, :] + sums) * scale).astype(jnp.bfloat16)
             slot[rows, :] = total if lower is None else jnp.where(lower, slot[rows, :], total)
 
-        column_block(earlies[1], rights[1], j, emit)
+        column_block(earlies[2], rights[1], j, emit)
         sums_copy(j).start()
         return carry
 
+    def join(slot, carry):
+        rows = pl.ds(pl.multiple_of(slot * share, share), share)
+        first_few, last_few = (earlies[part][rows, :].astype(jnp.float32) for part in range(2))
+        for pair in range(2):
+            some = slice(pair * few, (pair + 1) * few)
+            both = jnp.concatenate([first_few[some], last_few[some]], axis=0)
+            joined[rows, 2 * pair * R : 2 * (pair + 1) * R] = both.astype(jnp.bfloat16)
+        return carry
+
     arrive(0)
+    arrive(1)
+    lax.fori_loop(0, groups, join, 0)
     lax.fori_loop(0, columns, first_column, 0)
-    arrive(1)
+    arrive(2)
     lax.fori_loop(0, columns, second_column, 0)
     sums_copy(columns - 2).wait()
     sums_copy(columns - 1).wait()
 
     sent = blocks.at[pl.ds(0, N_TIME - 1)]
     pltpu.make_async_copy(sent, sent, send_times).wait()
-    for part in range(len(PARTS)):
+    for part in range(N_PARTS):
         sent = outgoing[part].at[pl.ds(0, groups - 1)]
         pltpu.make_async_copy(sent, sent, send_spectra.at[part]).wait()
-    arrive(len(PARTS) - 1)
+    arrive(N_PARTS - 1)
 
 
 def column_block(left, right, j, emit):
@@ -372,7 +397,7 @@
     late, early_sums = pl.pallas_call(
         functools.partial(channel_kernel, scale),
         out_shape=[
-            jax.ShapeDtypeStruct((signals, PARTS[-1] * R), jnp.bfloat16),
+            jax.ShapeDtypeStruct((signals, 2 * R), jnp.bfloat16),
             jax.ShapeDtypeStruct((signals, signals), jnp.bfloat16),
         ],
         in_specs=[in_hbm] * 7,
@@ -389,17 +414,18 @@
             pltpu.VMEM((filter_taps.shape[0] * R, R), jnp.float32),
             pltpu.VMEM((2, share, HALF, R), jnp.float32),
             pltpu.VMEM((N_TIME * 2 * share * HALF, R), jnp.float32),
-            [pltpu.VMEM((groups, share, part * R), jnp.bfloat16) for part in PARTS],
-            [pltpu.VMEM((signals, part * R), jnp.bfloat16) for part in PARTS[:2]],
-            [pltpu.VMEM((part * R, block), jnp.bfloat16) for part in PARTS[:2]],
+            [pltpu.VMEM((groups, share, 2 * R), jnp.bfloat16)] * N_PARTS,
+            [pltpu.VMEM((signals, 2 * R), jnp.bfloat16)] * (N_PARTS - 1),
+            pltpu.VMEM((signals, 4 * R), jnp.bfloat16),
+            [pltpu.VMEM((depth, block), jnp.bfloat16) for depth in (4 * R, 2 * R)],
             pltpu.VMEM((signals // block, signals, block), jnp.float32),
             pltpu.VMEM((2, signals, block), jnp.bfloat16),
             pltpu.SemaphoreType.DMA((3 + len(tables),)),
             pltpu.SemaphoreType.DMA((N_TIME,)),
             pltpu.SemaphoreType.DMA,
             pltpu.SemaphoreType.DMA((pieces,)),
-            pltpu.SemaphoreType.DMA((len(PARTS),)),
-            pltpu.SemaphoreType.DMA((len(PARTS),)),
+            pltpu.SemaphoreType.DMA((N_PARTS,)),
+            pltpu.SemaphoreType.DMA((N_PARTS,)),
             pltpu.SemaphoreType.DMA((2,)),
             pltpu.SemaphoreType.REGULAR,
         ],
@@ -413,8 +439,8 @@
         in_specs=[in_hbm, in_hbm],
         out_specs=in_hbm,
         scratch_shapes=[
-            pltpu.VMEM((signals, PARTS[-1] * R), jnp.bfloat16),
-            pltpu.VMEM((PARTS[-1] * R, last_block), jnp.bfloat16),
+            pltpu.VMEM((signals, 2 * R), jnp.bfloat16),
+            pltpu.VMEM((2 * R, last_block), jnp.bfloat16),
             pltpu.VMEM((signals // last_block, signals, last_block), jnp.bfloat16),
             pltpu.VMEM((signals // last_block, signals, last_block), jnp.bfloat16),
             pltpu.SemaphoreType.DMA,

time: 116 us -> 114 us (0.983); the launches traced: 116 us -> 112 us
  Pallas kernels: 116 us -> 112 us
    pallas_call x1, Pallas kernels: 108 us -> 104 us  [shards(): pl.pallas_call(functools.partial(channel_kernel, scale), out_shape=[jax.S...]
where the time goes in v5:
time: 114 us; the launch traced here: 112 us
  Pallas kernels  112 us (98%)
    pallas_call x1, Pallas kernels, shards(): pl.pallas_call(functools.partial(channel_kernel, scale), out_shape=[jax.S...  104 us
    pallas_call x1, Pallas kernels, shards(): pl.pallas_call(functools.partial(correlate_kernel, scale), out_shape=jax....  8.37 us

profile of v5, /device:TPU:1, one launch (start us, length us, event | category | flops | bytes accessed | tf_op | source)
XLA Modules:
  0.0 112.2 jit_solution(10848694062786380278)
XLA Ops:
  0.0 103.9 %channels.1 = (bf16[2048,256]{1,0:T(8,128)(2,1)}, bf16[2048,2048]{1,0:T(8,128)(2,1)}) custom-call(bf16[128,16384]{1,0:T(8,128)(2,1)} %volts.1, s32[128]{0:T(128)} %delays_in.1, s32[128]{0:T(128)} %dead_in.1, f32[4,16384]{1,0:T(4,128)} %taps_in.1, bf16[256,128]{1,0:T(8,128)(2,1)} %constant.6.clone.first_in, f32[2,128,128]{2,1,0:T(8,128)} %constant.7.clone.twist_in, ...), custom_call_target="tpu_custom_call" | custom-call | tf_op jit(solution)/shard_map/channels/pallas_call | solution.py:397
  103.9 8.4 %correlate.1 = bf16[1,2048,2048]{2,1,0:T(8,128)(2,1)} custom-call(bf16[2048,256]{1,0:T(8,128)(2,1)} %get-tuple-element.7.late, bf16[2048,2048]{1,0:T(8,128)(2,1)} %get-tuple-element.8.early_sums), custom_call_target="tpu_custom_call" | custom-call | tf_op jit(solution)/shard_map/correlate/pallas_call | solution.py:436

commit v6 on v5

--- a/solution.py
+++ b/solution.py
@@ -68,8 +68,8 @@
         lax.fori_loop(1, size, one, 0)
 
     def partner(step):
-        along_y = (3 * step) % 4
-        across = step % 2 * (1 - step // 4) + (1 - step % 2) * (step // 4)
+        along_y = step % 4
+        across = step // 4
         return (tm // 4 + across) % 2 * 4 + (tm + along_y) % 4
 
     def rows_of(owner):
@@ -389,7 +389,7 @@
     signals = signals_here * N_CHAN
     groups = N_TIME * N_CHAN
     in_hbm = pl.BlockSpec(memory_space=pltpu.HBM)
-    pieces = 16
+    pieces = 8
     block, last_block = 512, 512
     scale = 1.0 / (HALF * N_TIME)
     tables = dft_tables()

time: 114 us -> 112 us (0.982); the launches traced: 112 us -> 112 us
  no operation moved by 1% of the time
where the time goes in v6:
time: 112 us
  Pallas kernels  112 us (100%)
    pallas_call x1, Pallas kernels, shards(): pl.pallas_call(functools.partial(channel_kernel, scale), out_shape=[jax.S...  104 us
    pallas_call x1, Pallas kernels, shards(): pl.pallas_call(functools.partial(correlate_kernel, scale), out_shape=jax....  8.37 us

profile of v6, /device:TPU:1, one launch (start us, length us, event | category | flops | bytes accessed | tf_op | source)
XLA Modules:
  0.0 112.3 jit_solution(63933900545526647)
XLA Ops:
  0.0 104.0 %channels.1 = (bf16[2048,256]{1,0:T(8,128)(2,1)}, bf16[2048,2048]{1,0:T(8,128)(2,1)}) custom-call(bf16[128,16384]{1,0:T(8,128)(2,1)} %volts.1, s32[128]{0:T(128)} %delays_in.1, s32[128]{0:T(128)} %dead_in.1, f32[4,16384]{1,0:T(4,128)} %taps_in.1, bf16[256,128]{1,0:T(8,128)(2,1)} %constant.6.clone.first_in, f32[2,128,128]{2,1,0:T(8,128)} %constant.7.clone.twist_in, ...), custom_call_target="tpu_custom_call" | custom-call | tf_op jit(solution)/shard_map/channels/pallas_call | solution.py:397
  104.0 8.4 %correlate.1 = bf16[1,2048,2048]{2,1,0:T(8,128)(2,1)} custom-call(bf16[2048,256]{1,0:T(8,128)(2,1)} %get-tuple-element.7.late, bf16[2048,2048]{1,0:T(8,128)(2,1)} %get-tuple-element.8.early_sums), custom_call_target="tpu_custom_call" | custom-call | tf_op jit(solution)/shard_map/correlate/pallas_call | solution.py:436

commit v7 on v6

--- a/solution.py
+++ b/solution.py
@@ -325,13 +325,15 @@
 
 def column_block(left, right, j, emit):
     signals, depth = left.shape
-    block = right.shape[1]
+    block = right.shape[0]
     tall = signals
     here = pl.ds(pl.multiple_of(j * block, block), block)
-    right[...] = left[here, :].T
+    right[...] = left[here, :]
 
     def product(rows):
-        return jnp.dot(left[rows, :], right[...], preferred_element_type=jnp.float32)
+        return lax.dot_general(
+            left[rows, :], right[...], (((1,), (1,)), ((), ())), preferred_element_type=jnp.float32
+        )
 
     for m in range(signals // tall):
         rows = pl.ds(m * tall, tall)
@@ -348,7 +350,7 @@
 
 
 def correlate_kernel(scale, late, early_sums, out, left, right, sums_in, result, late_sem, in_sem, out_sem):
-    block = right.shape[1]
+    block = right.shape[0]
     columns = out.shape[2] // block
 
     def columns_of(j):
@@ -417,7 +419,7 @@
             [pltpu.VMEM((groups, share, 2 * R), jnp.bfloat16)] * N_PARTS,
             [pltpu.VMEM((signals, 2 * R), jnp.bfloat16)] * (N_PARTS - 1),
             pltpu.VMEM((signals, 4 * R), jnp.bfloat16),
-            [pltpu.VMEM((depth, block), jnp.bfloat16) for depth in (4 * R, 2 * R)],
+            [pltpu.VMEM((block, depth), jnp.bfloat16) for depth in (4 * R, 2 * R)],
             pltpu.VMEM((signals // block, signals, block), jnp.float32),
             pltpu.VMEM((2, signals, block), jnp.bfloat16),
             pltpu.SemaphoreType.DMA((3 + len(tables),)),
@@ -440,7 +442,7 @@
         out_specs=in_hbm,
         scratch_shapes=[
             pltpu.VMEM((signals, 2 * R), jnp.bfloat16),
-            pltpu.VMEM((2 * R, last_block), jnp.bfloat16),
+            pltpu.VMEM((last_block, 2 * R), jnp.bfloat16),
             pltpu.VMEM((signals // last_block, signals, last_block), jnp.bfloat16),
             pltpu.VMEM((signals // last_block, signals, last_block), jnp.bfloat16),
             pltpu.SemaphoreType.DMA,

time: 112 us -> 112 us (level)
  no operation moved by 1% of the time
where the time goes in v7:
time: 112 us
  Pallas kernels  112 us (100%)
    pallas_call x1, Pallas kernels, shards(): pl.pallas_call(functools.partial(channel_kernel, scale), out_shape=[jax.S...  104 us
    pallas_call x1, Pallas kernels, shards(): pl.pallas_call(functools.partial(correlate_kernel, scale), out_shape=jax....  8.14 us

profile of v7, /device:TPU:1, one launch (start us, length us, event | category | flops | bytes accessed | tf_op | source)
XLA Modules:
  0.0 112.1 jit_solution(3573323291756028666)
XLA Ops:
  0.0 104.0 %channels.1 = (bf16[2048,256]{1,0:T(8,128)(2,1)}, bf16[2048,2048]{1,0:T(8,128)(2,1)}) custom-call(bf16[128,16384]{1,0:T(8,128)(2,1)} %volts.1, s32[128]{0:T(128)} %delays_in.1, s32[128]{0:T(128)} %dead_in.1, f32[4,16384]{1,0:T(4,128)} %taps_in.1, bf16[256,128]{1,0:T(8,128)(2,1)} %constant.6.clone.first_in, f32[2,128,128]{2,1,0:T(8,128)} %constant.7.clone.twist_in, ...), custom_call_target="tpu_custom_call" | custom-call | tf_op jit(solution)/shard_map/channels/pallas_call | solution.py:399
  104.0 8.1 %correlate.1 = bf16[1,2048,2048]{2,1,0:T(8,128)(2,1)} custom-call(bf16[2048,256]{1,0:T(8,128)(2,1)} %get-tuple-element.7.late, bf16[2048,2048]{1,0:T(8,128)(2,1)} %get-tuple-element.8.early_sums), custom_call_target="tpu_custom_call" | custom-call | tf_op jit(solution)/shard_map/correlate/pallas_call | solution.py:438
